TPU v7x, 256 devices: a whole 4x4x8 slice. The times are simulated.
256 devices in a mesh: ctx: 256 (over z, x, y, core).
Axes of the slice: x: 4, y: 4, z: 8, core: 2. Of those that a mesh axis runs over, the one named last changes fastest.
Arguments:
- queries: bfloat16 [65536, 2048], P('ctx'), may hold values from -6 to 6
- key_rows: bfloat16 [65536, 2048], P('ctx'), may hold values from -6 to 6
- value_rows: bfloat16 [65536, 2048], P('ctx'), may hold values from -6 to 6
- token_rates: float32 [65536], P('ctx'), may hold values from 0.0001953125 to 0.001953125
- fast_weights: bfloat16 [4, 3, 512, 512], replicated, may hold values from -0.25 to 0.25
- out_gain: float32 [4, 512], replicated, may hold values from 0.1 to 0.4
- proj_weight: bfloat16 [2048, 2048], P(None, 'ctx'), may hold values from -0.125 to 0.125
Outputs:
- layer_out: bfloat16 [65536, 2048], P('ctx')
All inputs are finite; a program needn't handle non-finite values.
Results may differ from a plain program's by a relative error of at most 0.013.
Values may be sent and summed in bfloat16 or wider, within the bound.
A program may use at most 128 MiB of HBM per device.

v0:
```python
import jax
import jax.numpy as jnp
from jax import lax
from jax.sharding import PartitionSpec as P

WINDOW = 256


epsilon = 1e-06


def from_behind(value, axis, by):
    size = lax.axis_size(axis)
    pairs = [(i, i + by) for i in range(size) if 0 <= i + by < size]
    return lax.ppermute(value, axis, pairs)


def renorm_rows(weights, grads):
    shifted = weights - grads
    target = jnp.sqrt(jnp.mean(weights * weights, axis=-1, keepdims=True) + epsilon)
    current = jnp.sqrt(jnp.mean(shifted * shifted, axis=-1, keepdims=True) + epsilon)
    return shifted * (target / current)


def contract_rows(left, right):
    return lax.dot_general(
        left, right, (((0,), (0,)), ((), ())), preferred_element_type=jnp.float32
    )


def head_grads(keys, values, token_rates, weights_bf):
    pre_gate = jnp.dot(keys, weights_bf[0], preferred_element_type=jnp.float32)
    pre_up = jnp.dot(keys, weights_bf[2], preferred_element_type=jnp.float32)
    gate_sig = jax.nn.sigmoid(pre_gate)
    hidden = (pre_gate * gate_sig * pre_up).astype(jnp.bfloat16)
    out_grad = (-token_rates[:, None] * values.astype(jnp.float32)).astype(jnp.bfloat16)
    grad_down = contract_rows(hidden, out_grad)
    hidden_grad = lax.dot_general(
        out_grad, weights_bf[1], (((1,), (1,)), ((), ())), preferred_element_type=jnp.float32
    )
    gate_grad = (hidden_grad * pre_up * gate_sig * (1.0 + pre_gate * (1.0 - gate_sig))).astype(
        jnp.bfloat16
    )
    up_grad = (hidden_grad * pre_gate * gate_sig).astype(jnp.bfloat16)
    grad_gate = contract_rows(keys, gate_grad)
    grad_up = contract_rows(keys, up_grad)
    return jnp.stack([grad_gate, grad_down, grad_up])


def head_forward(query_part, updated, gain):
    query_gate = jnp.dot(query_part, updated[0], preferred_element_type=jnp.float32)
    query_up = jnp.dot(query_part, updated[2], preferred_element_type=jnp.float32)
    fast_hidden = (jax.nn.silu(query_gate) * query_up).astype(jnp.bfloat16)
    fast_out = jnp.dot(fast_hidden, updated[1], preferred_element_type=jnp.float32)
    return (
        fast_out * lax.rsqrt(jnp.mean(fast_out * fast_out, axis=-1, keepdims=True) + epsilon) * gain
    )


def head_attend(query_part, key_extended, value_extended, global_first):
    tok_rows = query_part.shape[0]
    head_width = query_part.shape[1]
    block_rows = min(512, tok_rows)
    blocks_count = tok_rows // block_rows
    score_scale = head_width ** (-0.5)
    row_pos = lax.broadcasted_iota(jnp.int32, (block_rows, block_rows + WINDOW), 0)
    col_pos = lax.broadcasted_iota(jnp.int32, (block_rows, block_rows + WINDOW), 1)

    def one_block(block_index):
        first = block_index * block_rows
        scores = (
            lax.dot_general(
                query_part,
                key_extended,
                (((1,), (1,)), ((), ())),
                preferred_element_type=jnp.float32,
            )
            * score_scale
        )
        valid = (
            (col_pos > row_pos)
            & (col_pos <= row_pos + WINDOW)
            & (global_first + first + col_pos - WINDOW >= 0)
        )
        scores = jnp.where(valid, scores, -1e30)
        top = jnp.max(scores, axis=-1, keepdims=True)
        expd = jnp.where(valid, jnp.exp(scores - top), 0.0)
        prob_rows = (expd / jnp.sum(expd, axis=-1, keepdims=True)).astype(jnp.bfloat16)
        return jnp.dot(prob_rows, value_extended, preferred_element_type=jnp.float32)

    return lax.map(one_block, jnp.arange(blocks_count, dtype=jnp.int32)).reshape(
        tok_rows, head_width
    )


def body(queries, key_rows, value_rows, token_rates, fast_weights, out_gain, proj_weight):
    tok_rows = queries.shape[0]
    head_count = fast_weights.shape[0]
    head_width = fast_weights.shape[2]
    tail_rows = from_behind((key_rows, value_rows), "ctx", 1)
    grads = []
    for head in range(head_count):
        cols = slice(head * head_width, (head + 1) * head_width)
        grads.append(
            head_grads(key_rows[:, cols], value_rows[:, cols], token_rates, fast_weights[head])
        )
    stacked = jnp.stack(grads).reshape(head_count * 3 * head_width, head_width)
    flat_weights = fast_weights.astype(jnp.float32).reshape(head_count * 3 * head_width, head_width)
    shares = lax.psum_scatter(stacked, "ctx", scatter_dimension=0, tiled=True)
    row_count = shares.shape[0]
    own_rows = lax.dynamic_slice_in_dim(
        flat_weights, lax.axis_index("ctx") * row_count, row_count, 0
    )
    fresh = renorm_rows(own_rows, shares).astype(jnp.bfloat16)
    updated = lax.all_gather(fresh, "ctx", axis=0, tiled=True).reshape(
        head_count, 3, head_width, head_width
    )
    key_extended = jnp.concatenate([tail_rows[0], key_rows], axis=0)
    value_extended = jnp.concatenate([tail_rows[1], value_rows], axis=0)
    global_first = lax.axis_index("ctx") * tok_rows
    pieces = []
    for head in range(head_count):
        cols = slice(head * head_width, (head + 1) * head_width)
        normed = head_forward(queries[:, cols], updated[head], out_gain[head])
        attended = head_attend(
            queries[:, cols], key_extended[:, cols], value_extended[:, cols], global_first
        )
        pieces.append((attended + normed).astype(jnp.bfloat16))
    combined = jnp.concatenate(pieces, axis=1)
    whole_proj = lax.all_gather(proj_weight, "ctx", axis=1, tiled=True)
    projected = jnp.dot(combined, whole_proj, preferred_element_type=jnp.float32)
    return projected.astype(jnp.bfloat16)


def solution(mesh):
    return jax.shard_map(
        body,
        mesh=mesh,
        in_specs=(
            P("ctx", None),
            P("ctx", None),
            P("ctx", None),
            P("ctx"),
            P(),
            P(),
            P(None, "ctx"),
        ),
        out_specs=P("ctx", None),
        check_vma=False,
    )
```

profile of v0, /device:TPU:1, one launch (start us, length us, event | category | flops | bytes accessed | tf_op | source)
XLA Modules:
  0.0 694.1 jit_solution(2635363211593658865)
XLA Ops:
  6.5 1.5 fusion.73
  8.1 1.5 fusion.75
  10.3 1.5 fusion.77
  11.7 1.5 fusion.71
  13.2 1.4 fusion.67
  14.6 1.3 fusion.69
  24.2 1.2 maximum_bitcast_fusion
  25.4 1.4 maximum_bitcast_fusion.2
  26.8 5.0 pad_maximum_fusion
  31.9 406.6 %reduce-scatter.2.cloned.1.call-done = f32[24,512]{1,0:T(8,128)} async-done(((f32[6144,512]{1,0:T(8,128)}), f32[24,512]{1,0:T(8,128)}) %reduce-scatter.2.cloned.1.call-update) | async-done | bytes 49168 | tf_op jit(solution)/shard_map/reduce_scatter | solution.py:109
  439.4 1.5 multiply_convert_fusion.36
  441.7 7.8 %collective-permute-start = (bf16[256,2048]{1,0:T(8,128)(2,1)S(1)}, bf16[256,2048]{1,0:T(8,128)(2,1)}, u32[]{:S(2)}, u32[]{:S(2)}) collective-permute-start(bf16[256,2048]{1,0:T(8,128)(2,1)S(1)} %copy-done), channel_id=1, source_target_pairs={{0,1},{1,2},{2,3},{3,4},{4,5},{5,6},{6,7},{7,8},{8,9},{9,10},{10,1... | collective-permute-start | bytes 3145736 | tf_op jit(solution)/shard_map/ppermute | solution.py:15
  449.4 2.1 collective-permute-start.1
  451.6 9.6 %collective-permute-done = bf16[256,2048]{1,0:T(8,128)(2,1)} collective-permute-done((bf16[256,2048]{1,0:T(8,128)(2,1)S(1)}, bf16[256,2048]{1,0:T(8,128)(2,1)}, u32[]{:S(2)}, u32[]{:S(2)}) %collective-permute-start) | collective-permute-done | bytes 1048608 | tf_op jit(solution)/shard_map/ppermute | solution.py:15
  461.3 1.3 constant_dynamic-update-slice_fusion.1
  464.5 8.1 %collective-permute-done.1 = bf16[256,2048]{1,0:T(8,128)(2,1)} collective-permute-done((bf16[256,2048]{1,0:T(8,128)(2,1)S(1)}, bf16[256,2048]{1,0:T(8,128)(2,1)}, u32[]{:S(2)}, u32[]{:S(2)}) %collective-permute-start.1) | collective-permute-done | bytes 1048608 | tf_op jit(solution)/shard_map/ppermute | solution.py:15
  472.7 2.3 constant_dynamic-update-slice_fusion.3
  476.1 85.2 %all-gather.3.cloned.1.call-done = bf16[6144,512]{1,0:T(8,128)(2,1)} async-done(((bf16[24,512]{1,0:T(8,128)(2,1)}), bf16[6144,512]{1,0:T(8,128)(2,1)}) %all-gather.3.cloned.1.call-update) | async-done | bytes 6291472 | tf_op jit(solution)/shard_map/all_gather | solution.py:115
  561.2 1.3 convolution_bitcast_fusion.19
  562.6 2.5 multiply_reduce_fusion.3
  565.1 1.3 convolution_bitcast_fusion.17
  566.4 2.5 multiply_reduce_fusion.2
  569.0 1.3 convolution_bitcast_fusion.15
  570.3 2.5 multiply_reduce_fusion.1
  572.9 1.4 convolution_bitcast_fusion.13
  574.3 2.5 multiply_reduce_fusion
  576.8 1.9 fusion.12
  578.7 1.6 fusion.13
  580.4 1.5 fusion.14
  581.9 1.5 fusion.15
  583.4 97.4 %all-gather.5.cloned.1.call-done = bf16[2048,2048]{0,1:T(8,128)(2,1)} async-done(((bf16[2048,8]{0,1:T(8,128)(2,1)}), bf16[2048,2048]{0,1:T(8,128)(2,1)}) %all-gather.5.cloned.1.call-update) | async-done | bytes 8388624 | tf_op jit(solution)/shard_map/all_gather | solution.py:130
  680.8 6.8 convolution_convert_fusion
  (64 shorter events, 13.6 us)
Async XLA Ops:
  6.5 8.1 %copy-start = (bf16[256,2048]{1,0:T(8,128)(2,1)S(1)}, bf16[256,2048]{1,0:T(8,128)(2,1)}, u32[]{:S(2)}) copy-start(bf16[256,2048]{1,0:T(8,128)(2,1)} %param.8) | copy-start | bytes 3145732
  6.5 431.9 %reduce-scatter.2.cloned.1.call-start = ((), (), s32[]{:S(2)}) async-start(), calls=%async_computation.1 | async-start | bytes 12632064 | tf_op jit(solution)/shard_map/reduce_scatter | solution.py:109
  8.1 8.9 %copy-start.2 = (bf16[256,2048]{1,0:T(8,128)(2,1)S(1)}, bf16[256,2048]{1,0:T(8,128)(2,1)}, u32[]{:S(2)}) copy-start(bf16[256,2048]{1,0:T(8,128)(2,1)} %param.9) | copy-start | bytes 3145732
  16.4 2.3 slice-start
  17.4 2.2 slice-start.1
  31.8 419.8 %copy-start.6 = (f32[4,512]{1,0:T(4,128)S(1)}, f32[4,512]{1,0:T(4,128)}, u32[]{:S(2)}) copy-start(f32[4,512]{1,0:T(4,128)} %param.12) | copy-start | bytes 24580
  31.8 430.8 %copy-start.1 = (bf16[256,2048]{1,0:T(8,128)(2,1)S(1)}, bf16[256,2048]{1,0:T(8,128)(2,1)}, u32[]{:S(2)}) copy-start(bf16[256,2048]{1,0:T(8,128)(2,1)} %param.7) | copy-start | bytes 3145732
  31.8 529.4 %all-gather.3.cloned.1.call-start = ((), (), s32[]{:S(2)}) async-start(), calls=%async_computation.2 | async-start | bytes 6316032 | tf_op jit(solution)/shard_map/all_gather | solution.py:115
  440.9 239.9 %all-gather.5.cloned.1.call-start = ((), (), s32[]{:S(2)}) async-start(), calls=%async_computation.3 | async-start | bytes 8421376 | tf_op jit(solution)/shard_map/all_gather | solution.py:130
  441.7 19.6 %collective-permute-start = (bf16[256,2048]{1,0:T(8,128)(2,1)S(1)}, bf16[256,2048]{1,0:T(8,128)(2,1)}, u32[]{:S(2)}, u32[]{:S(2)}) collective-permute-start(bf16[256,2048]{1,0:T(8,128)(2,1)S(1)} %copy-done), channel_id=1, source_target_pairs={{0,1},{1,2},{2,3},{3,4},{4,5},{5,6},{6,7},{7,8},{8,9},{9,10},{10,1... | collective-permute-start | bytes 3145736 | tf_op jit(solution)/shard_map/ppermute | solution.py:15
  449.4 23.2 %collective-permute-start.1 = (bf16[256,2048]{1,0:T(8,128)(2,1)S(1)}, bf16[256,2048]{1,0:T(8,128)(2,1)}, u32[]{:S(2)}, u32[]{:S(2)}) collective-permute-start(bf16[256,2048]{1,0:T(8,128)(2,1)S(1)} %copy-done.2), channel_id=1, source_target_pairs={{0,1},{1,2},{2,3},{3,4},{4,5},{5,6},{6,7},{7,8},{8,9},{9,10},{10,1... | collective-permute-start | bytes 3145736 | tf_op jit(solution)/shard_map/ppermute | solution.py:15
  463.7 11.2 %copy-start.5 = (f32[256,512]{0,1:T(8,128)}, f32[256,512]{0,1:T(8,128)S(1)}, u32[]{:S(2)}) copy-start(f32[256,512]{0,1:T(8,128)S(1)} %get-tuple-element.96) | copy-start | bytes 1572868
  464.1 8.5 %copy-start.3 = (f32[256,512]{0,1:T(8,128)}, f32[256,512]{0,1:T(8,128)S(1)}, u32[]{:S(2)}) copy-start(f32[256,512]{0,1:T(8,128)S(1)} %get-tuple-element.98) | copy-start | bytes 1572868
  572.9 5.9 copy-start.4
  576.8 3.6 copy-start.8
  576.8 5.1 copy-start.7
Sparse Core Ops, SparseCore 0:
  32.0 406.4 reduce-scatter.1
  442.3 118.8 all-gather.2
  565.0 115.7 all-gather.4
where the time goes:
time: 695 us; the launch traced here: 694 us
  waiting for transfers between devices  608 us (87%)
  matrix products  46.2 us (7%)
  between operations  13.5 us (2%)
  other arithmetic  11.2 us (2%)
  starting transfers between devices  9.97 us (1%)
    reduce_scatter x1, waiting for transfers between devices, body(): shares = lax.psum_scatter(stacked, 'ctx', scatter_dimension=0, tiled=True)  407 us
    all_gather x1, waiting for transfers between devices, body(): whole_proj = lax.all_gather(proj_weight, 'ctx', axis=1, tiled=True)  97.4 us
    all_gather x1, waiting for transfers between devices, body(): lax.all_gather(fresh, 'ctx', axis=0, tiled=True)  85.2 us
    ppermute x2, waiting for transfers between devices, from_behind(): return lax.ppermute(value, axis, pairs)  17.8 us
  transfers between devices with their start and end apart: 5, of which 5 were waited for; matrix products, arithmetic and copies ran while one was open for 4% of the time, Pallas kernels for 0%

commit v1 on v0

v1 whole, which is shorter than its diff:
```python
import functools

import jax
import jax.numpy as jnp
from jax import lax
from jax.experimental import pallas as pl
from jax.experimental.pallas import tpu as pltpu
from jax.sharding import PartitionSpec as P

HD = 512
TOK = 256
EPS = 1e-06
F32 = jnp.float32
BF16 = jnp.bfloat16
MESH = pl.DeviceIdType.MESH


def mm(a, b):
    return jnp.dot(a, b, preferred_element_type=F32)


def mm_nt(a, b):
    return lax.dot_general(a, b, (((1,), (1,)), ((), ())), preferred_element_type=F32)


def mm_tn(a, b):
    return lax.dot_general(a, b, (((0,), (0,)), ((), ())), preferred_element_type=F32)


def aligned(index, step):
    return pl.multiple_of(index * step, step)


def kernel(
    q_hbm, k_hbm, v_hbm, rates_ref, w_hbm, gain_ref, proj_ref, out_hbm,
    qb, kb, vb, wb, rates_st, rates_sib, pst, prx, pj,
    pg, pu, hg, og, hid, gg, ug,
    gb, ra, rb, fl, fr, sec, rsec, zacc, w32, zs, rz, agz, wn,
    att, comb, osend, orecv, obuf,
    loc_sem, sib_send, sib_recv, prim_send, prim_recv, sec_send, sec_recv,
    z_send, z_recv, agz_send, agz_recv, agsec_send, agsec_recv, agp_send, agp_recv,
    py_send, py_recv, px_send, px_recv, pz_send, pz_recv, halo_send, halo_recv,
    os_send, os_recv, out_sem,
):
    me = lax.axis_index("ctx")
    core = lax.rem(me, 2)
    chip = lax.div(me, 2)
    y = lax.rem(chip, 4)
    x = lax.rem(lax.div(chip, 4), 4)
    z = lax.div(chip, 16)
    sib = me + 1 - 2 * core
    p = core * y + (1 - core) * x
    s = core * x + (1 - core) * y
    p_step = 8 - 6 * core
    s_step = 2 + 6 * core

    def along(position, size, step, by):
        return me + (lax.rem(position + by, size) - position) * step

    right = along(p, 4, p_step, 1)
    left = along(p, 4, p_step, 3)
    z_right = along(z, 8, 32, 1)
    z_left = along(z, 8, 32, 7)
    nxt = lax.rem(me + 2, 256)
    prv = lax.rem(me + 254, 256)

    def remote(src, dst, send, recv, device):
        return pltpu.make_async_remote_copy(
            src_ref=src, dst_ref=dst, send_sem=send, recv_sem=recv,
            device_id=(device,), device_id_type=MESH,
        )

    pending = []

    def go(copies):
        for copy in copies:
            copy.start()
            pending.append(copy)
        return copies

    mine = pl.ds(aligned(core, 1024), 1024)
    theirs = pl.ds(aligned(1 - core, 1024), 1024)
    my_rows = aligned(core, TOK)
    locals_ = [
        pltpu.make_async_copy(k_hbm.at[:, mine], kb.at[pl.ds(256 + my_rows, TOK), :], loc_sem.at[0]),
        pltpu.make_async_copy(w_hbm.at[pl.ds(2 * core, 2)], wb, loc_sem.at[1]),
        pltpu.make_async_copy(v_hbm.at[:, mine], vb.at[pl.ds(256 + my_rows, TOK), :], loc_sem.at[2]),
        pltpu.make_async_copy(q_hbm.at[:, mine], qb.at[pl.ds(my_rows, TOK), :], loc_sem.at[3]),
    ]
    for copy in locals_:
        copy.start()

    barrier = pltpu.get_barrier_semaphore()
    partners = [sib, nxt, prv]
    partners += [along(x, 4, 8, d) for d in (1, 2, 3)]
    partners += [along(y, 4, 2, d) for d in (1, 2, 3)]
    partners += [along(z, 8, 32, d) for d in range(1, 8)]
    for device in partners:
        pl.semaphore_signal(barrier, inc=1, device_id=(device,), device_id_type=MESH)

    rates_st[0:2, :] = rates_ref[...]
    rates_st[2:8, :] = jnp.zeros((6, 128), F32)
    shard = proj_ref[...].astype(F32)
    first_core = core == 0
    own_half = jnp.where(first_core, shard[:, :1024], shard[:, 1024:])
    sib_half = jnp.where(first_core, shard[:, 1024:], shard[:, :1024])
    pst[...] = jnp.concatenate([sib_half, sib_half], axis=0).astype(BF16)

    pl.semaphore_wait(barrier, len(partners))

    to_sib = [
        (pst, prx),
        (rates_st, rates_sib),
        (k_hbm.at[:, theirs], kb.at[pl.ds(256 + my_rows, TOK), :]),
        (v_hbm.at[:, theirs], vb.at[pl.ds(256 + my_rows, TOK), :]),
        (q_hbm.at[:, theirs], qb.at[pl.ds(my_rows, TOK), :]),
    ]
    sib_copies = go([
        remote(src, dst, sib_send.at[i], sib_recv.at[i], sib)
        for i, (src, dst) in enumerate(to_sib)
    ])

    def grads_rows(j, block, rates):
        cols = slice(j * HD, (j + 1) * HD)
        rows = aligned(block, TOK)
        keys = kb[pl.ds(256 + rows, TOK), cols]
        for i in range(2):
            rate = jnp.transpose(jnp.broadcast_to(rates[i:i + 1, :], (128, 128)))
            rate = jnp.concatenate([rate] * 4, axis=1)
            values = vb[pl.ds(256 + rows + i * 128, 128), cols].astype(F32)
            og[j, pl.ds(rows + i * 128, 128), :] = (-rate * values).astype(BF16)
        pg[...] = mm(keys, wb[j, 0])
        pu[...] = mm(keys, wb[j, 2])
        hg[...] = mm_nt(og[j, pl.ds(rows, TOK), :], wb[j, 1])

        def step(i, carry):
            part = pl.ds(aligned(i, 32), 32)
            dest = pl.ds(rows + aligned(i, 32), 32)
            gate, up, grad = pg[part, :], pu[part, :], hg[part, :]
            sig = jax.nn.sigmoid(gate)
            act = gate * sig
            hid[j, dest, :] = (act * up).astype(BF16)
            gg[j, dest, :] = (grad * up * sig * (1.0 + gate * (1.0 - sig))).astype(BF16)
            ug[j, dest, :] = (grad * act).astype(BF16)
            return carry

        lax.fori_loop(0, 8, step, 0)

    def grads_sum(j):
        def step(i, carry):
            lanes = pl.ds(pl.multiple_of(j * HD + i * 256, 256), 256)
            out = pl.ds(aligned(i, 256), 256)
            keys = kb[256:768, lanes]
            gb[3 * j, out, :] = mm_tn(keys, gg[j]).astype(BF16)
            gb[3 * j + 2, out, :] = mm_tn(keys, ug[j]).astype(BF16)
            gb[3 * j + 1, out, :] = mm_tn(hid[j, :, pl.ds(aligned(i, 256), 256)], og[j]).astype(BF16)
            return carry

        lax.fori_loop(0, 2, step, 0)

    def chunk_rows(by, part):
        start = lax.rem(p + by, 4) * 128 + part * 64
        return pl.ds(pl.multiple_of(start, 64), 64)

    def prim_first(j):
        mats = pl.ds(3 * j, 3)
        moves = [
            (gb.at[mats, chunk_rows(2, 0), :], ra.at[mats], right),
            (gb.at[mats, chunk_rows(2, 1), :], rb.at[mats], left),
            (gb.at[mats, chunk_rows(1, 1), :], fl.at[mats, 64:128, :], right),
            (gb.at[mats, chunk_rows(3, 0), :], fr.at[mats, 0:64, :], left),
        ]
        return go([
            remote(src, dst, prim_send.at[6 * j + i], prim_recv.at[6 * j + i], dev)
            for i, (src, dst, dev) in enumerate(moves)
        ])

    def add_into(j, rows, extra):
        for m in range(3 * j, 3 * j + 3):
            total = gb[m, rows, :].astype(F32) + extra[m].astype(F32)
            gb[m, rows, :] = total.astype(BF16)

    def prim_second(j, first):
        mats = pl.ds(3 * j, 3)
        first[0].wait_recv()
        add_into(j, chunk_rows(1, 0), ra)
        a = remote(gb.at[mats, chunk_rows(1, 0), :], fl.at[mats, 0:64, :],
                   prim_send.at[6 * j + 4], prim_recv.at[6 * j + 4], right)
        go([a])
        first[1].wait_recv()
        add_into(j, chunk_rows(3, 1), rb)
        b = remote(gb.at[mats, chunk_rows(3, 1), :], fr.at[mats, 64:128, :],
                   prim_send.at[6 * j + 5], prim_recv.at[6 * j + 5], left)
        go([b])
        return [first[2], first[3], a, b]

    def prim_last(j, copies):
        for copy in copies:
            copy.wait_recv()

        def step(i, carry):
            rows = pl.ds(aligned(i, 32), 32)
            own = pl.ds(pl.multiple_of(p * 128 + i * 32, 32), 32)
            for m in range(3 * j, 3 * j + 3):
                total = gb[m, own, :].astype(F32) + fl[m, rows, :].astype(F32)
                sec[m, rows, :] = (total + fr[m, rows, :].astype(F32)).astype(BF16)
            return carry

        lax.fori_loop(0, 4, step, 0)

    def sec_sends(j):
        mats = pl.ds(3 * j, 3)
        out = []
        for d in (1, 2, 3):
            rows = pl.ds(aligned(lax.rem(s + d, 4), 32), 32)
            out.append(remote(sec.at[mats, rows, :], rsec.at[d - 1, mats],
                              sec_send.at[3 * j + d - 1], sec_recv.at[3 * j + d - 1],
                              along(s, 4, s_step, d)))
        return go(out)

    def sec_last(j, copies):
        for copy in copies:
            copy.wait_recv()
        own = pl.ds(aligned(s, 32), 32)
        for m in range(3 * j, 3 * j + 3):
            total = sec[m, own, :].astype(F32)
            for d in range(3):
                total = total + rsec[d, m].astype(F32)
            zacc[32 * m:32 * m + 32, :] = total

    def z_sends():
        for owner in range(8):
            for i in range(3):
                rows = slice(24 * owner + 8 * i, 24 * owner + 8 * i + 8)
                both = jnp.concatenate([zacc[rows, 0:256], zacc[rows, 256:512]], axis=0)
                zs[owner, :, i * 256:(i + 1) * 256] = both.astype(BF16)
        return go([
            remote(zs.at[lax.rem(z + d, 8)], rz.at[d - 1], z_send.at[d - 1], z_recv.at[d - 1],
                   along(z, 8, 32, d))
            for d in range(1, 8)
        ])

    def renorm(copies):
        for copy in copies:
            copy.wait_recv()
        for i in range(3):
            lanes = slice(i * 256, (i + 1) * 256)
            total = rz[0, :, lanes].astype(F32)
            for d in range(1, 7):
                total = total + rz[d, :, lanes].astype(F32)
            rows = pl.ds(pl.multiple_of(24 * z + 8 * i, 8), 8)
            grad = zacc[rows, :] + jnp.concatenate([total[0:8], total[8:16]], axis=1)
            weights = w32[rows, :]
            shifted = weights - grad
            target = jnp.sqrt(jnp.mean(weights * weights, axis=-1, keepdims=True) + EPS)
            current = jnp.sqrt(jnp.mean(shifted * shifted, axis=-1, keepdims=True) + EPS)
            fresh = shifted * (target / current)
            both = jnp.concatenate([fresh[:, 0:256], fresh[:, 256:512]], axis=0)
            agz[z, :, lanes] = both.astype(BF16)
        return go([
            remote(agz.at[z], agz.at[z], agz_send.at[d - 1], agz_recv.at[d - 1],
                   along(z, 8, 32, d))
            for d in range(1, 8)
        ])

    own_block = pl.ds(pl.multiple_of(128 * p + 32 * s, 32), 32)

    def unpack(copies):
        for copy in copies:
            copy.wait_recv()
        for m in range(6):
            groups = []
            for g in range(4 * m, 4 * m + 4):
                both = agz[g // 3, :, (g % 3) * 256:(g % 3 + 1) * 256].astype(F32)
                groups.append(jnp.concatenate([both[0:8], both[8:16]], axis=1))
            wn[m, own_block, :] = jnp.concatenate(groups, axis=0).astype(BF16)

    def agsec_sends(j):
        part = wn.at[pl.ds(3 * j, 3), own_block, :]
        return go([
            remote(part, part, agsec_send.at[3 * j + d - 1], agsec_recv.at[3 * j + d - 1],
                   along(s, 4, s_step, d))
            for d in (1, 2, 3)
        ])

    def agp_first(j):
        mats = pl.ds(3 * j, 3)
        half_a = wn.at[mats, chunk_rows(0, 0), :]
        half_b = wn.at[mats, chunk_rows(0, 1), :]
        moves = [(half_a, right), (half_b, left), (half_b, right), (half_a, left)]
        return go([
            remote(ref, ref, agp_send.at[6 * j + i], agp_recv.at[6 * j + i], dev)
            for i, (ref, dev) in enumerate(moves)
        ])

    def agp_second(j, first):
        mats = pl.ds(3 * j, 3)
        first[0].wait_recv()
        half_a = wn.at[mats, chunk_rows(3, 0), :]
        a = remote(half_a, half_a, agp_send.at[6 * j + 4], agp_recv.at[6 * j + 4], right)
        go([a])
        first[1].wait_recv()
        half_b = wn.at[mats, chunk_rows(1, 1), :]
        b = remote(half_b, half_b, agp_send.at[6 * j + 5], agp_recv.at[6 * j + 5], left)
        go([b])
        return [first[2], first[3], a, b]

    def attend(j, block):
        cols = slice(j * HD, (j + 1) * HD)
        first = block * TOK
        pg[...] = mm_nt(qb[first:first + TOK, cols], kb[first:first + 2 * TOK, cols])

        def step(i, carry):
            part = pl.ds(aligned(i, 32), 32)
            row = lax.broadcasted_iota(jnp.int32, (32, 512), 0) + i * 32
            col = lax.broadcasted_iota(jnp.int32, (32, 512), 1)
            valid = (col > row) & (col <= row + 256)
            if block == 0:
                valid = valid & (chip * 512 + col >= 256)
            scores = jnp.where(valid, pg[part, :] * (HD ** -0.5), -1e30)
            top = jnp.max(scores, axis=-1, keepdims=True)
            expd = jnp.exp(scores - top)
            probs = expd / jnp.sum(expd, axis=-1, keepdims=True)
            gg[0, part, :] = probs.astype(BF16)
            return carry

        lax.fori_loop(0, 8, step, 0)
        att[first:first + TOK, cols] = mm(gg[0, 0:TOK, :], vb[first:first + 2 * TOK, cols])

    def forward(j):
        cols = slice(j * HD, (j + 1) * HD)
        gain = gain_ref[pl.ds(2 * core + j, 1), :]

        def block(b, carry):
            rows = aligned(b, TOK)
            queries = qb[pl.ds(rows, TOK), cols]
            pg[...] = mm(queries, wn[3 * j])
            pu[...] = mm(queries, wn[3 * j + 2])

            def act(i, inner):
                part = pl.ds(aligned(i, 32), 32)
                gate = pg[part, :]
                gg[0, part, :] = (gate * jax.nn.sigmoid(gate) * pu[part, :]).astype(BF16)
                return inner

            lax.fori_loop(0, 8, act, 0)
            hg[...] = mm(gg[0, 0:TOK, :], wn[3 * j + 1])

            def norm(i, inner):
                part = pl.ds(aligned(i, 32), 32)
                dest = pl.ds(rows + aligned(i, 32), 32)
                fast = hg[part, :]
                scale = lax.rsqrt(jnp.mean(fast * fast, axis=-1, keepdims=True) + EPS)
                comb[dest, cols] = (att[dest, cols] + fast * scale * gain).astype(BF16)
                return inner

            lax.fori_loop(0, 8, norm, 0)
            return carry

        lax.fori_loop(0, 2, block, 0)

    for copy in locals_[:3]:
        copy.wait()
    for j in range(2):
        grads_rows(j, core, rates_ref[...])

    sib_copies[0].wait_recv()
    received = prx[...].astype(F32)[0:8]
    pair = jnp.concatenate(
        [jnp.where(first_core, own_half, received), jnp.where(first_core, received, own_half)], axis=0
    )
    pj[pl.ds(aligned(chip, 16), 16), :] = pair.astype(BF16)
    part = pj.at[pl.ds(aligned(chip, 16), 16), :]
    py = go([
        remote(part, part, py_send.at[d - 1], py_recv.at[d - 1], along(y, 4, 2, d))
        for d in (1, 2, 3)
    ])

    for copy in sib_copies[1:4]:
        copy.wait_recv()
    grads_rows(0, 1 - core, rates_sib[...])
    grads_sum(0)
    prim0 = prim_first(0)

    for copy in py:
        copy.wait_recv()
    part = pj.at[pl.ds(aligned(lax.div(chip, 4), 64), 64), :]
    px = go([
        remote(part, part, px_send.at[d - 1], px_recv.at[d - 1], along(x, 4, 8, d))
        for d in (1, 2, 3)
    ])

    grads_rows(1, 1 - core, rates_sib[...])
    grads_sum(1)
    prim1 = prim_first(1)
    prim0 = prim_second(0, prim0)

    def plane(by, lo=0, size=256):
        start = lax.rem(z + by, 8) * 256 + lo
        return pj.at[pl.ds(pl.multiple_of(start, 128), size), :]

    def pz(step, by_right, by_left, lo_right=0, lo_left=0, size=256):
        a = plane(by_right, lo_right, size)
        b = plane(by_left, lo_left, size)
        return go([
            remote(a, a, pz_send.at[2 * step], pz_recv.at[2 * step], z_right),
            remote(b, b, pz_send.at[2 * step + 1], pz_recv.at[2 * step + 1], z_left),
        ])

    for copy in px:
        copy.wait_recv()
    pz0 = pz(0, 0, 0)

    locals_[3].wait()
    sib_copies[4].wait_recv()
    attend(0, 1)
    prim1 = prim_second(1, prim1)
    prim_last(0, prim0)
    sec0 = sec_sends(0)

    for m in range(6):
        w32[32 * m:32 * m + 32, :] = wb[m // 3, m % 3, own_block, :].astype(F32)
    attend(1, 1)

    prim_last(1, prim1)
    sec1 = sec_sends(1)
    halo = go([
        remote(buf.at[512:768, :], buf.at[0:256, :], halo_send.at[i], halo_recv.at[i], nxt)
        for i, buf in enumerate((kb, vb))
    ])
    sec_last(0, sec0)
    sec_last(1, sec1)
    zc = z_sends()
    for copy in pz0:
        copy.wait_recv()
    pz1 = pz(1, 7, 1)
    ag = renorm(zc)
    unpack(ag)
    ags0 = agsec_sends(0)
    ags1 = agsec_sends(1)
    for copy in ags0:
        copy.wait_recv()
    agp0 = agp_first(0)
    for copy in ags1:
        copy.wait_recv()
    agp1 = agp_first(1)
    for copy in halo:
        copy.wait_recv()
    attend(0, 0)
    agp0 = agp_second(0, agp0)
    for copy in pz1:
        copy.wait_recv()
    pz2 = pz(2, 6, 2)
    attend(1, 0)
    agp1 = agp_second(1, agp1)
    for copy in agp0:
        copy.wait_recv()
    forward(0)
    for copy in pz2:
        copy.wait_recv()
    pz3 = pz(3, 5, 3, 0, 128, 128)
    for copy in agp1:
        copy.wait_recv()
    forward(1)
    for copy in pz3:
        copy.wait_recv()

    def partial(rows, n):
        return mm_nt(comb[pl.ds(rows, TOK), :], pj[pl.ds(n * 512, 512), :])

    outs = []
    for n in range(4):
        osend[n] = partial(aligned(1 - core, TOK), n).astype(BF16)
        outs += go([remote(osend.at[n], orecv.at[n], os_send.at[n], os_recv.at[n], sib)])
    finals = []
    for n in range(4):
        total = partial(my_rows, n)
        outs[n].wait_recv()
        obuf[n] = (total + orecv[n].astype(F32)).astype(BF16)
        copy = pltpu.make_async_copy(obuf.at[n], out_hbm.at[:, n * 512:(n + 1) * 512], out_sem.at[n])
        copy.start()
        finals.append(copy)
    for copy in pending:
        copy.wait_send()
    for copy in finals:
        copy.wait()


def body(queries, key_rows, value_rows, token_rates, fast_weights, out_gain, proj_weight):
    anywhere = pl.BlockSpec(memory_space=pl.ANY)
    vmem = pl.BlockSpec(memory_space=pltpu.VMEM)
    sem = pltpu.SemaphoreType.DMA
    scratch = [
        pltpu.VMEM((512, 1024), BF16),
        pltpu.VMEM((768, 1024), BF16),
        pltpu.VMEM((768, 1024), BF16),
        pltpu.VMEM((2, 3, 512, 512), BF16),
        pltpu.VMEM((8, 128), F32),
        pltpu.VMEM((8, 128), F32),
        pltpu.VMEM((16, 1024), BF16),
        pltpu.VMEM((16, 1024), BF16),
        pltpu.VMEM((2048, 1024), BF16),
        pltpu.VMEM((256, 512), F32),
        pltpu.VMEM((256, 512), F32),
        pltpu.VMEM((256, 512), F32),
        pltpu.VMEM((2, 512, 512), BF16),
        pltpu.VMEM((2, 512, 512), BF16),
        pltpu.VMEM((2, 512, 512), BF16),
        pltpu.VMEM((2, 512, 512), BF16),
        pltpu.VMEM((6, 512, 512), BF16),
        pltpu.VMEM((6, 64, 512), BF16),
        pltpu.VMEM((6, 64, 512), BF16),
        pltpu.VMEM((6, 128, 512), BF16),
        pltpu.VMEM((6, 128, 512), BF16),
        pltpu.VMEM((6, 128, 512), BF16),
        pltpu.VMEM((3, 6, 32, 512), BF16),
        pltpu.VMEM((192, 512), F32),
        pltpu.VMEM((192, 512), F32),
        pltpu.VMEM((8, 16, 768), BF16),
        pltpu.VMEM((7, 16, 768), BF16),
        pltpu.VMEM((8, 16, 768), BF16),
        pltpu.VMEM((6, 512, 512), BF16),
        pltpu.VMEM((512, 1024), F32),
        pltpu.VMEM((512, 1024), BF16),
        pltpu.VMEM((4, 256, 512), BF16),
        pltpu.VMEM((4, 256, 512), BF16),
        pltpu.VMEM((4, 256, 512), BF16),
        sem((4,)),
        sem((5,)), sem((5,)),
        sem((12,)), sem((12,)),
        sem((6,)), sem((6,)),
        sem((7,)), sem((7,)),
        sem((7,)), sem((7,)),
        sem((6,)), sem((6,)),
        sem((12,)), sem((12,)),
        sem((3,)), sem((3,)),
        sem((3,)), sem((3,)),
        sem((8,)), sem((8,)),
        sem((2,)), sem((2,)),
        sem((4,)), sem((4,)),
        sem((4,)),
    ]
    return pl.pallas_call(
        kernel,
        out_shape=jax.ShapeDtypeStruct((TOK, 2048), BF16),
        in_specs=[anywhere, anywhere, anywhere, vmem, anywhere, vmem, vmem],
        out_specs=anywhere,
        scratch_shapes=scratch,
        compiler_params=pltpu.CompilerParams(
            collective_id=0, has_side_effects=True, vmem_limit_bytes=56 * 1024 * 1024
        ),
        cost_estimate=pl.CostEstimate(flops=12 * 10**9, bytes_accessed=10**7, transcendentals=10**6),
    )(
        queries, key_rows, value_rows, token_rates.reshape(2, 128), fast_weights, out_gain,
        proj_weight.T,
    )


def solution(mesh):
    return jax.shard_map(
        body,
        mesh=mesh,
        in_specs=(
            P("ctx", None),
            P("ctx", None),
            P("ctx", None),
            P("ctx"),
            P(),
            P(),
            P(None, "ctx"),
        ),
        out_specs=P("ctx", None),
        check_vma=False,
    )
```

time: 695 us -> 119 us (0.17)
  waiting for transfers between devices: 608 us -> 0 us
  Pallas kernels: 0 us -> 117 us
  matrix products: 46.2 us -> 0 us
  between operations: 13.5 us -> 0.01 us
  other arithmetic: 11.2 us -> 0 us
  starting transfers between devices: 9.97 us -> 0 us
    reduce_scatter x1 -> x0, waiting for transfers between devices: 407 us -> none  [body(): shares = lax.psum_scatter(stacked, 'ctx', scatter_dimension=0, tiled=True)]
    all_gather x2 -> x0, waiting for transfers between devices: 183 us -> none  [the longest x1 97.4 us: body(): whole_proj = lax.all_gather(proj_weight, 'ctx', axis=1, tiled=True)]
    pallas_call x0 -> x1, Pallas kernels: none -> 117 us  [body(): pl.pallas_call(kernel, out_shape=jax.ShapeDtypeStruct((TOK, 2048), BF16),...]
    dot_general x41 -> x0, matrix products: 46.2 us -> none  [the longest x4 10.1 us: head_forward(): jnp.dot(fast_hidden, updated[1], preferred_element_type=jnp.float32)]
    ppermute x2 -> x0, waiting for transfers between devices: 17.8 us -> none  [from_behind(): return lax.ppermute(value, axis, pairs)]
    ppermute x2 -> x0, starting transfers between devices: 9.88 us -> none  [from_behind(): return lax.ppermute(value, axis, pairs)]
    another operation x3 -> x0, other arithmetic: 7.59 us -> none  [body(): stacked = jnp.stack(grads).reshape(head_count * 3 * head_width, head_width)]
  transfers between devices with their start and end apart: 5 -> 0, of which waited for: 5 -> 0; matrix products, arithmetic and copies ran while one was open for 4% -> 0% of each run, Pallas kernels for 0% -> 0%
where the time goes in v1:
time: 119 us
  Pallas kernels  117 us (98%)
  local copies, waits for them, and re-layouts  2.3 us (2%)
    pallas_call x1, Pallas kernels, body(): pl.pallas_call(kernel, out_shape=jax.ShapeDtypeStruct((TOK, 2048), BF16),...  117 us

profile of v1, /device:TPU:1, one launch (start us, length us, event | category | flops | bytes accessed | tf_op | source)
XLA Modules:
  0.0 119.3 jit_solution(16701082778115846754)
XLA Ops:
  0.0 117.0 %shard_map.73 = bf16[256,2048]{1,0:T(8,128)(2,1)} custom-call(bf16[256,2048]{1,0:T(8,128)(2,1)} %q_hbm.1, bf16[256,2048]{1,0:T(8,128)(2,1)} %k_hbm.1, bf16[256,2048]{1,0:T(8,128)(2,1)} %v_hbm.1, f32[2,128]{1,0:T(2,128)} %bitcast.3, bf16[4,3,512,512]{3,2,1,0:T(8,128)(2,1)} %w_hbm.1, f32[4,512]{1,0:T(4,128)} %gain_ref.1, bf16[8,2048]{1,0:T(8,128)(2,1)} %bitcast.2), custom_call_target="tpu_custom_call" | custom-call | flops 12000000000 | bytes 10000000 | tf_op jit(solution)/shard_map/pallas_call | solution.py:543
  117.0 2.3 %copy.9 = bf16[256,2048]{1,0:T(8,128)(2,1)} copy(bf16[256,2048]{1,0:T(8,128)(2,1)} %shard_map.73) | data formatting | bytes 2097152

commit v2 on v1

--- a/solution.py
+++ b/solution.py
@@ -10,6 +10,7 @@
 HD = 512
 TOK = 256
 EPS = 1e-06
+CUT = 768
 F32 = jnp.float32
 BF16 = jnp.bfloat16
 MESH = pl.DeviceIdType.MESH
@@ -32,15 +33,16 @@
 
 
 def kernel(
-    q_hbm, k_hbm, v_hbm, rates_ref, w_hbm, gain_ref, proj_ref, out_hbm,
+    q_hbm, k_hbm, v_hbm, rates_ref, w_hbm, gain_ref, proj_ref, out_ref,
     qb, kb, vb, wb, rates_st, rates_sib, pst, prx, pj,
     pg, pu, hg, og, hid, gg, ug,
-    gb, ra, rb, fl, fr, sec, rsec, zacc, w32, zs, rz, agz, wn,
-    att, comb, osend, orecv, obuf,
+    gb, ra, rb, fl, fr, sec, rsec, zacc, wpk, zs, rz, agz, wn,
+    att, comb, acc, osend, orecv,
     loc_sem, sib_send, sib_recv, prim_send, prim_recv, sec_send, sec_recv,
     z_send, z_recv, agz_send, agz_recv, agsec_send, agsec_recv, agp_send, agp_recv,
-    py_send, py_recv, px_send, px_recv, pz_send, pz_recv, halo_send, halo_recv,
-    os_send, os_recv, out_sem,
+    py_send, py_recv, px_send, px_recv, pz_send, pz_recv,
+    bz_send, bz_recv, by_send, by_recv, bx_send, bx_recv, halo_send, halo_recv,
+    os_send, os_recv,
 ):
     me = lax.axis_index("ctx")
     core = lax.rem(me, 2)
@@ -222,58 +224,62 @@
         for copy in copies:
             copy.wait_recv()
         own = pl.ds(aligned(s, 32), 32)
-        for m in range(3 * j, 3 * j + 3):
-            total = sec[m, own, :].astype(F32)
+        for m in range(3):
+            total = sec[3 * j + m, own, :].astype(F32)
             for d in range(3):
-                total = total + rsec[d, m].astype(F32)
-            zacc[32 * m:32 * m + 32, :] = total
-
-    def z_sends():
-        for owner in range(8):
-            for i in range(3):
-                rows = slice(24 * owner + 8 * i, 24 * owner + 8 * i + 8)
-                both = jnp.concatenate([zacc[rows, 0:256], zacc[rows, 256:512]], axis=0)
-                zs[owner, :, i * 256:(i + 1) * 256] = both.astype(BF16)
+                total = total + rsec[d, 3 * j + m].astype(F32)
+            zacc[j, 32 * m:32 * m + 32, :] = total
+
+    def pack(j, out):
+        for group in range(24):
+            rows = zacc[j, 4 * group:4 * group + 4, :]
+            tall = jnp.concatenate([rows[:, c * 128:(c + 1) * 128] for c in range(4)], axis=0)
+            lanes = slice(group % 3 * 128, (group % 3 + 1) * 128)
+            out[j, group // 3, :, lanes] = tall.astype(BF16)
+
+    def z_sends(j):
+        pack(j, zs)
         return go([
-            remote(zs.at[lax.rem(z + d, 8)], rz.at[d - 1], z_send.at[d - 1], z_recv.at[d - 1],
+            remote(zs.at[j, lax.rem(z + d, 8)], rz.at[j, d - 1],
+                   z_send.at[7 * j + d - 1], z_recv.at[7 * j + d - 1], along(z, 8, 32, d))
+            for d in range(1, 8)
+        ])
+
+    def renorm(j, copies):
+        for copy in copies:
+            copy.wait_recv()
+
+        def rms(tall):
+            square = tall * tall
+            square = square[0:4] + square[4:8] + square[8:12] + square[12:16]
+            return jnp.sqrt(jnp.sum(square, axis=-1, keepdims=True) * (1.0 / HD) + EPS)
+
+        for i in range(3):
+            lanes = slice(i * 128, (i + 1) * 128)
+            grad = zs[j, z, :, lanes].astype(F32)
+            for d in range(7):
+                grad = grad + rz[j, d, :, lanes].astype(F32)
+            weights = wpk[j, z, :, lanes].astype(F32)
+            shifted = weights - grad
+            scale = rms(weights) / rms(shifted)
+            agz[j, z, :, lanes] = (shifted * jnp.concatenate([scale] * 4, axis=0)).astype(BF16)
+        return go([
+            remote(agz.at[j, z], agz.at[j, z], agz_send.at[7 * j + d - 1], agz_recv.at[7 * j + d - 1],
                    along(z, 8, 32, d))
             for d in range(1, 8)
         ])
 
-    def renorm(copies):
+    own_block = pl.ds(pl.multiple_of(128 * p + 32 * s, 32), 32)
+
+    def unpack(j, copies):
         for copy in copies:
             copy.wait_recv()
-        for i in range(3):
-            lanes = slice(i * 256, (i + 1) * 256)
-            total = rz[0, :, lanes].astype(F32)
-            for d in range(1, 7):
-                total = total + rz[d, :, lanes].astype(F32)
-            rows = pl.ds(pl.multiple_of(24 * z + 8 * i, 8), 8)
-            grad = zacc[rows, :] + jnp.concatenate([total[0:8], total[8:16]], axis=1)
-            weights = w32[rows, :]
-            shifted = weights - grad
-            target = jnp.sqrt(jnp.mean(weights * weights, axis=-1, keepdims=True) + EPS)
-            current = jnp.sqrt(jnp.mean(shifted * shifted, axis=-1, keepdims=True) + EPS)
-            fresh = shifted * (target / current)
-            both = jnp.concatenate([fresh[:, 0:256], fresh[:, 256:512]], axis=0)
-            agz[z, :, lanes] = both.astype(BF16)
-        return go([
-            remote(agz.at[z], agz.at[z], agz_send.at[d - 1], agz_recv.at[d - 1],
-                   along(z, 8, 32, d))
-            for d in range(1, 8)
-        ])
-
-    own_block = pl.ds(pl.multiple_of(128 * p + 32 * s, 32), 32)
-
-    def unpack(copies):
-        for copy in copies:
-            copy.wait_recv()
-        for m in range(6):
-            groups = []
-            for g in range(4 * m, 4 * m + 4):
-                both = agz[g // 3, :, (g % 3) * 256:(g % 3 + 1) * 256].astype(F32)
-                groups.append(jnp.concatenate([both[0:8], both[8:16]], axis=1))
-            wn[m, own_block, :] = jnp.concatenate(groups, axis=0).astype(BF16)
+        for m in range(3):
+            rows = []
+            for g in range(8 * m, 8 * m + 8):
+                tall = agz[j, g // 3, :, g % 3 * 128:(g % 3 + 1) * 128].astype(F32)
+                rows.append(jnp.concatenate([tall[4 * c:4 * c + 4] for c in range(4)], axis=1))
+            wn[3 * j + m, own_block, :] = jnp.concatenate(rows, axis=0).astype(BF16)
 
     def agsec_sends(j):
         part = wn.at[pl.ds(3 * j, 3), own_block, :]
@@ -311,9 +317,9 @@
         pg[...] = mm_nt(qb[first:first + TOK, cols], kb[first:first + 2 * TOK, cols])
 
         def step(i, carry):
-            part = pl.ds(aligned(i, 32), 32)
-            row = lax.broadcasted_iota(jnp.int32, (32, 512), 0) + i * 32
-            col = lax.broadcasted_iota(jnp.int32, (32, 512), 1)
+            part = pl.ds(aligned(i, 64), 64)
+            row = lax.broadcasted_iota(jnp.int32, (64, 512), 0) + i * 64
+            col = lax.broadcasted_iota(jnp.int32, (64, 512), 1)
             valid = (col > row) & (col <= row + 256)
             if block == 0:
                 valid = valid & (chip * 512 + col >= 256)
@@ -324,7 +330,7 @@
             gg[0, part, :] = probs.astype(BF16)
             return carry
 
-        lax.fori_loop(0, 8, step, 0)
+        lax.fori_loop(0, 4, step, 0)
         att[first:first + TOK, cols] = mm(gg[0, 0:TOK, :], vb[first:first + 2 * TOK, cols])
 
     def forward(j):
@@ -338,23 +344,23 @@
             pu[...] = mm(queries, wn[3 * j + 2])
 
             def act(i, inner):
-                part = pl.ds(aligned(i, 32), 32)
+                part = pl.ds(aligned(i, 64), 64)
                 gate = pg[part, :]
                 gg[0, part, :] = (gate * jax.nn.sigmoid(gate) * pu[part, :]).astype(BF16)
                 return inner
 
-            lax.fori_loop(0, 8, act, 0)
+            lax.fori_loop(0, 4, act, 0)
             hg[...] = mm(gg[0, 0:TOK, :], wn[3 * j + 1])
 
             def norm(i, inner):
-                part = pl.ds(aligned(i, 32), 32)
-                dest = pl.ds(rows + aligned(i, 32), 32)
+                part = pl.ds(aligned(i, 64), 64)
+                dest = pl.ds(rows + aligned(i, 64), 64)
                 fast = hg[part, :]
                 scale = lax.rsqrt(jnp.mean(fast * fast, axis=-1, keepdims=True) + EPS)
                 comb[dest, cols] = (att[dest, cols] + fast * scale * gain).astype(BF16)
                 return inner
 
-            lax.fori_loop(0, 8, norm, 0)
+            lax.fori_loop(0, 4, norm, 0)
             return carry
 
         lax.fori_loop(0, 2, block, 0)
@@ -369,121 +375,150 @@
     pair = jnp.concatenate(
         [jnp.where(first_core, own_half, received), jnp.where(first_core, received, own_half)], axis=0
     )
-    pj[pl.ds(aligned(chip, 16), 16), :] = pair.astype(BF16)
-    part = pj.at[pl.ds(aligned(chip, 16), 16), :]
+    lanes_a, lanes_b = slice(0, CUT), slice(CUT, 1024)
+    spot = 4 * x + y
+    place = pl.ds(aligned(spot, 16), 16)
+    pj[z, place, :] = pair.astype(BF16)
+
+    def same(ref, send, recv, device):
+        return remote(ref, ref, send, recv, device)
+
     py = go([
-        remote(part, part, py_send.at[d - 1], py_recv.at[d - 1], along(y, 4, 2, d))
+        same(pj.at[z, place, lanes_a], py_send.at[d - 1], py_recv.at[d - 1], along(y, 4, 2, d))
         for d in (1, 2, 3)
     ])
-
-    for copy in sib_copies[1:4]:
-        copy.wait_recv()
+    bz = go([
+        same(pj.at[z, place, lanes_b], bz_send.at[d - 1], bz_recv.at[d - 1], along(z, 8, 32, d))
+        for d in range(1, 8)
+    ])
+
+    def settle(copies):
+        for copy in copies:
+            copy.wait_recv()
+
+    def pz(step, by_right, by_left, lo_right=0, lo_left=0, size=256):
+        a = pj.at[lax.rem(z + by_right, 8), lo_right:lo_right + size, lanes_a]
+        b = pj.at[lax.rem(z + by_left, 8), lo_left:lo_left + size, lanes_a]
+        return go([
+            same(a, pz_send.at[2 * step], pz_recv.at[2 * step], z_right),
+            same(b, pz_send.at[2 * step + 1], pz_recv.at[2 * step + 1], z_left),
+        ])
+
+    x_right = along(x, 4, 8, 1)
+    x_left = along(x, 4, 8, 3)
+
+    def strip(by, half):
+        start = lax.rem(x + by, 4) * 64 + half * 32
+        return pj.at[:, pl.ds(pl.multiple_of(start, 32), 32), lanes_b]
+
+    def bx(step, moves):
+        return go([
+            same(strip(by_, half), bx_send.at[4 * step + i], bx_recv.at[4 * step + i], dev)
+            for i, (by_, half, dev) in enumerate(moves)
+        ])
+
+    def halo(i):
+        buf, lanes = [(kb, slice(0, 512)), (kb, slice(512, 1024)), (vb, slice(0, 512)), (vb, slice(512, 1024))][i]
+        return go([remote(buf.at[512:768, lanes], buf.at[0:256, lanes],
+                          halo_send.at[i], halo_recv.at[i], nxt)])
+
+    settle(sib_copies[1:3])
+    halo_k = halo(0)
+    settle(sib_copies[3:4])
     grads_rows(0, 1 - core, rates_sib[...])
     grads_sum(0)
     prim0 = prim_first(0)
 
-    for copy in py:
-        copy.wait_recv()
-    part = pj.at[pl.ds(aligned(lax.div(chip, 4), 64), 64), :]
+    settle(py)
+    part = pj.at[z, pl.ds(aligned(x, 64), 64), lanes_a]
     px = go([
-        remote(part, part, px_send.at[d - 1], px_recv.at[d - 1], along(x, 4, 8, d))
-        for d in (1, 2, 3)
+        same(part, px_send.at[d - 1], px_recv.at[d - 1], along(x, 4, 8, d)) for d in (1, 2, 3)
     ])
-
+    settle(bz)
+    part = pj.at[:, place, lanes_b]
+    by = go([
+        same(part, by_send.at[d - 1], by_recv.at[d - 1], along(y, 4, 2, d)) for d in (1, 2, 3)
+    ])
     grads_rows(1, 1 - core, rates_sib[...])
     grads_sum(1)
+    settle(px)
+    pz0 = pz(0, 0, 0)
+    prim0 = prim_second(0, prim0)
     prim1 = prim_first(1)
-    prim0 = prim_second(0, prim0)
-
-    def plane(by, lo=0, size=256):
-        start = lax.rem(z + by, 8) * 256 + lo
-        return pj.at[pl.ds(pl.multiple_of(start, 128), size), :]
-
-    def pz(step, by_right, by_left, lo_right=0, lo_left=0, size=256):
-        a = plane(by_right, lo_right, size)
-        b = plane(by_left, lo_left, size)
-        return go([
-            remote(a, a, pz_send.at[2 * step], pz_recv.at[2 * step], z_right),
-            remote(b, b, pz_send.at[2 * step + 1], pz_recv.at[2 * step + 1], z_left),
-        ])
-
-    for copy in px:
-        copy.wait_recv()
-    pz0 = pz(0, 0, 0)
-
+    for j in range(2):
+        for m in range(3):
+            zacc[j, 32 * m:32 * m + 32, :] = wb[j, m, own_block, :].astype(F32)
+        pack(j, wpk)
     locals_[3].wait()
-    sib_copies[4].wait_recv()
+    settle(sib_copies[4:5])
     attend(0, 1)
-    prim1 = prim_second(1, prim1)
     prim_last(0, prim0)
     sec0 = sec_sends(0)
-
-    for m in range(6):
-        w32[32 * m:32 * m + 32, :] = wb[m // 3, m % 3, own_block, :].astype(F32)
+    settle(pz0)
+    pz1 = pz(1, 7, 1)
+    prim1 = prim_second(1, prim1)
+    sec_last(0, sec0)
+    z0 = z_sends(0)
     attend(1, 1)
-
     prim_last(1, prim1)
     sec1 = sec_sends(1)
-    halo = go([
-        remote(buf.at[512:768, :], buf.at[0:256, :], halo_send.at[i], halo_recv.at[i], nxt)
-        for i, buf in enumerate((kb, vb))
-    ])
-    sec_last(0, sec0)
+    ag0 = renorm(0, z0)
+    halo_k += halo(1)
+    halo_v = halo(2)
+    settle(by)
+    bx0 = bx(0, [(0, 0, x_right), (0, 1, x_left), (0, 1, x_right), (0, 0, x_left)])
     sec_last(1, sec1)
-    zc = z_sends()
-    for copy in pz0:
-        copy.wait_recv()
-    pz1 = pz(1, 7, 1)
-    ag = renorm(zc)
-    unpack(ag)
+    z1 = z_sends(1)
+    unpack(0, ag0)
     ags0 = agsec_sends(0)
+    ag1 = renorm(1, z1)
+    settle(ags0)
+    agp0 = agp_first(0)
+    halo_v += halo(3)
+    settle(pz1)
+    pz2 = pz(2, 6, 2)
+    unpack(1, ag1)
     ags1 = agsec_sends(1)
-    for copy in ags0:
-        copy.wait_recv()
-    agp0 = agp_first(0)
-    for copy in ags1:
-        copy.wait_recv()
+    agp0 = agp_second(0, agp0)
+    settle(ags1)
     agp1 = agp_first(1)
-    for copy in halo:
-        copy.wait_recv()
+    settle(bx0)
+    bx1 = bx(1, [(3, 0, x_right), (1, 1, x_left)])
+    settle(pz2)
+    pz3 = pz(3, 5, 3, 0, 128, 128)
+    settle(halo_k)
+    settle(halo_v[:1])
     attend(0, 0)
-    agp0 = agp_second(0, agp0)
-    for copy in pz1:
-        copy.wait_recv()
-    pz2 = pz(2, 6, 2)
+    settle(halo_v[1:])
     attend(1, 0)
     agp1 = agp_second(1, agp1)
-    for copy in agp0:
-        copy.wait_recv()
+    settle(agp0)
     forward(0)
-    for copy in pz2:
-        copy.wait_recv()
-    pz3 = pz(3, 5, 3, 0, 128, 128)
-    for copy in agp1:
-        copy.wait_recv()
+    settle(pz3)
+    settle(bx1)
+
+    their_rows = aligned(1 - core, TOK)
+
+    def partial(rows, j, n):
+        return mm_nt(comb[pl.ds(rows, TOK), j * HD:(j + 1) * HD],
+                     jnp.concatenate([pj[2 * n, :, j * HD:(j + 1) * HD],
+                                      pj[2 * n + 1, :, j * HD:(j + 1) * HD]], axis=0))
+
+    for n in range(4):
+        acc[0, n] = partial(their_rows, 0, n)
+        acc[1, n] = partial(my_rows, 0, n)
+    settle(agp1)
     forward(1)
-    for copy in pz3:
-        copy.wait_recv()
-
-    def partial(rows, n):
-        return mm_nt(comb[pl.ds(rows, TOK), :], pj[pl.ds(n * 512, 512), :])
-
     outs = []
     for n in range(4):
-        osend[n] = partial(aligned(1 - core, TOK), n).astype(BF16)
+        osend[n] = (acc[0, n] + partial(their_rows, 1, n)).astype(BF16)
         outs += go([remote(osend.at[n], orecv.at[n], os_send.at[n], os_recv.at[n], sib)])
-    finals = []
     for n in range(4):
-        total = partial(my_rows, n)
+        total = acc[1, n] + partial(my_rows, 1, n)
         outs[n].wait_recv()
-        obuf[n] = (total + orecv[n].astype(F32)).astype(BF16)
-        copy = pltpu.make_async_copy(obuf.at[n], out_hbm.at[:, n * 512:(n + 1) * 512], out_sem.at[n])
-        copy.start()
-        finals.append(copy)
+        out_ref[:, n * 512:(n + 1) * 512] = (total + orecv[n].astype(F32)).astype(BF16)
     for copy in pending:
         copy.wait_send()
-    for copy in finals:
-        copy.wait()
 
 
 def body(queries, key_rows, value_rows, token_rates, fast_weights, out_gain, proj_weight):
@@ -499,7 +534,7 @@
         pltpu.VMEM((8, 128), F32),
         pltpu.VMEM((16, 1024), BF16),
         pltpu.VMEM((16, 1024), BF16),
-        pltpu.VMEM((2048, 1024), BF16),
+        pltpu.VMEM((8, 256, 1024), BF16),
         pltpu.VMEM((256, 512), F32),
         pltpu.VMEM((256, 512), F32),
         pltpu.VMEM((256, 512), F32),
@@ -514,37 +549,39 @@
         pltpu.VMEM((6, 128, 512), BF16),
         pltpu.VMEM((6, 128, 512), BF16),
         pltpu.VMEM((3, 6, 32, 512), BF16),
-        pltpu.VMEM((192, 512), F32),
-        pltpu.VMEM((192, 512), F32),
-        pltpu.VMEM((8, 16, 768), BF16),
-        pltpu.VMEM((7, 16, 768), BF16),
-        pltpu.VMEM((8, 16, 768), BF16),
+        pltpu.VMEM((2, 96, 512), F32),
+        pltpu.VMEM((2, 8, 16, 384), BF16),
+        pltpu.VMEM((2, 8, 16, 384), BF16),
+        pltpu.VMEM((2, 7, 16, 384), BF16),
+        pltpu.VMEM((2, 8, 16, 384), BF16),
         pltpu.VMEM((6, 512, 512), BF16),
         pltpu.VMEM((512, 1024), F32),
         pltpu.VMEM((512, 1024), BF16),
-        pltpu.VMEM((4, 256, 512), BF16),
+        pltpu.VMEM((2, 4, 256, 512), F32),
         pltpu.VMEM((4, 256, 512), BF16),
         pltpu.VMEM((4, 256, 512), BF16),
         sem((4,)),
         sem((5,)), sem((5,)),
         sem((12,)), sem((12,)),
         sem((6,)), sem((6,)),
-        sem((7,)), sem((7,)),
-        sem((7,)), sem((7,)),
+        sem((14,)), sem((14,)),
+        sem((14,)), sem((14,)),
         sem((6,)), sem((6,)),
         sem((12,)), sem((12,)),
         sem((3,)), sem((3,)),
         sem((3,)), sem((3,)),
         sem((8,)), sem((8,)),
-        sem((2,)), sem((2,)),
+        sem((7,)), sem((7,)),
+        sem((3,)), sem((3,)),
+        sem((8,)), sem((8,)),
         sem((4,)), sem((4,)),
-        sem((4,)),
+        sem((4,)), sem((4,)),
     ]
     return pl.pallas_call(
         kernel,
-        out_shape=jax.ShapeDtypeStruct((TOK, 2048), BF16),
+        out_shape=pltpu.VMEM((TOK, 2048), BF16),
         in_specs=[anywhere, anywhere, anywhere, vmem, anywhere, vmem, vmem],
-        out_specs=anywhere,
+        out_specs=vmem,
         scratch_shapes=scratch,
         compiler_params=pltpu.CompilerParams(
             collective_id=0, has_side_effects=True, vmem_limit_bytes=56 * 1024 * 1024

time: 119 us -> 100 us (0.84)
  Pallas kernels: 117 us -> 99.3 us
  local copies, waits for them, and re-layouts: 2.3 us -> 0.97 us
    pallas_call x1, Pallas kernels: 117 us -> 99.3 us  [body(): pl.pallas_call(kernel, out_shape=pltpu.VMEM((TOK, 2048), BF16), in_specs=...]
    unnamed x1, local copies, waits for them, and re-layouts: 2.3 us -> 0.97 us
where the time goes in v2:
time: 100 us
  Pallas kernels  99.3 us (99%)
    pallas_call x1, Pallas kernels, body(): pl.pallas_call(kernel, out_shape=pltpu.VMEM((TOK, 2048), BF16), in_specs=...  99.3 us

profile of v2, /device:TPU:1, one launch (start us, length us, event | category | flops | bytes accessed | tf_op | source)
XLA Modules:
  0.0 100.3 jit_solution(15037745518812750208)
XLA Ops:
  0.0 99.3 %shard_map.73 = bf16[256,2048]{1,0:T(8,128)(2,1)S(1)} custom-call(bf16[256,2048]{1,0:T(8,128)(2,1)} %q_hbm.1, bf16[256,2048]{1,0:T(8,128)(2,1)} %k_hbm.1, bf16[256,2048]{1,0:T(8,128)(2,1)} %v_hbm.1, f32[2,128]{1,0:T(2,128)} %bitcast.3, bf16[4,3,512,512]{3,2,1,0:T(8,128)(2,1)} %w_hbm.1, f32[4,512]{1,0:T(4,128)} %gain_ref.1, bf16[8,2048]{1,0:T(8,128)(2,1)} %bitcast.2), custom_call_target="tpu_custom_call" | custom-call | flops 12000000000 | bytes 10000000 | tf_op jit(solution)/shard_map/pallas_call | solution.py:580
  99.3 1.0 copy.9

commit v3 on v2

--- a/solution.py
+++ b/solution.py
@@ -10,7 +10,8 @@
 HD = 512
 TOK = 256
 EPS = 1e-06
-CUT = 768
+CUT = 896
+HALF = 32
 F32 = jnp.float32
 BF16 = jnp.bfloat16
 MESH = pl.DeviceIdType.MESH
@@ -161,16 +162,16 @@
         lax.fori_loop(0, 2, step, 0)
 
     def chunk_rows(by, part):
-        start = lax.rem(p + by, 4) * 128 + part * 64
-        return pl.ds(pl.multiple_of(start, 64), 64)
+        start = lax.rem(p + by, 4) * 128 + part * HALF
+        return pl.ds(pl.multiple_of(start, HALF), (HALF, 128 - HALF)[part])
 
     def prim_first(j):
         mats = pl.ds(3 * j, 3)
         moves = [
             (gb.at[mats, chunk_rows(2, 0), :], ra.at[mats], right),
             (gb.at[mats, chunk_rows(2, 1), :], rb.at[mats], left),
-            (gb.at[mats, chunk_rows(1, 1), :], fl.at[mats, 64:128, :], right),
-            (gb.at[mats, chunk_rows(3, 0), :], fr.at[mats, 0:64, :], left),
+            (gb.at[mats, chunk_rows(1, 1), :], fl.at[mats, HALF:128, :], right),
+            (gb.at[mats, chunk_rows(3, 0), :], fr.at[mats, 0:HALF, :], left),
         ]
         return go([
             remote(src, dst, prim_send.at[6 * j + i], prim_recv.at[6 * j + i], dev)
@@ -186,12 +187,12 @@
         mats = pl.ds(3 * j, 3)
         first[0].wait_recv()
         add_into(j, chunk_rows(1, 0), ra)
-        a = remote(gb.at[mats, chunk_rows(1, 0), :], fl.at[mats, 0:64, :],
+        a = remote(gb.at[mats, chunk_rows(1, 0), :], fl.at[mats, 0:HALF, :],
                    prim_send.at[6 * j + 4], prim_recv.at[6 * j + 4], right)
         go([a])
         first[1].wait_recv()
         add_into(j, chunk_rows(3, 1), rb)
-        b = remote(gb.at[mats, chunk_rows(3, 1), :], fr.at[mats, 64:128, :],
+        b = remote(gb.at[mats, chunk_rows(3, 1), :], fr.at[mats, HALF:128, :],
                    prim_send.at[6 * j + 5], prim_recv.at[6 * j + 5], left)
         go([b])
         return [first[2], first[3], a, b]
@@ -365,10 +366,6 @@
 
         lax.fori_loop(0, 2, block, 0)
 
-    for copy in locals_[:3]:
-        copy.wait()
-    for j in range(2):
-        grads_rows(j, core, rates_ref[...])
 
     sib_copies[0].wait_recv()
     received = prx[...].astype(F32)[0:8]
@@ -396,13 +393,15 @@
         for copy in copies:
             copy.wait_recv()
 
-    def pz(step, by_right, by_left, lo_right=0, lo_left=0, size=256):
-        a = pj.at[lax.rem(z + by_right, 8), lo_right:lo_right + size, lanes_a]
-        b = pj.at[lax.rem(z + by_left, 8), lo_left:lo_left + size, lanes_a]
-        return go([
-            same(a, pz_send.at[2 * step], pz_recv.at[2 * step], z_right),
-            same(b, pz_send.at[2 * step + 1], pz_recv.at[2 * step + 1], z_left),
-        ])
+    def pz(step, half, by_right, by_left, sides=(0, 1)):
+        blocks = (lax.rem(z + by_right, 8), lax.rem(z + by_left, 8))
+        rows = slice(128 * half, 128 * half + 128)
+        out = []
+        for side in sides:
+            ref = pj.at[blocks[side], rows, lanes_a]
+            i = 4 * step + 2 * half + side
+            out.append(same(ref, pz_send.at[i], pz_recv.at[i], (z_right, z_left)[side]))
+        return go(out)
 
     x_right = along(x, 4, 8, 1)
     x_left = along(x, 4, 8, 3)
@@ -413,27 +412,35 @@
 
     def bx(step, moves):
         return go([
-            same(strip(by_, half), bx_send.at[4 * step + i], bx_recv.at[4 * step + i], dev)
+            same(strip(by_, half), bx_send.at[2 * step + i], bx_recv.at[2 * step + i], dev)
             for i, (by_, half, dev) in enumerate(moves)
         ])
 
     def halo(i):
-        buf, lanes = [(kb, slice(0, 512)), (kb, slice(512, 1024)), (vb, slice(0, 512)), (vb, slice(512, 1024))][i]
+        buf = (kb, vb)[i // 4]
+        lanes = slice(i % 4 * 256, i % 4 * 256 + 256)
         return go([remote(buf.at[512:768, lanes], buf.at[0:256, lanes],
                           halo_send.at[i], halo_recv.at[i], nxt)])
 
+    for copy in locals_[:3]:
+        copy.wait()
+    grads_rows(0, core, rates_ref[...])
     settle(sib_copies[1:3])
-    halo_k = halo(0)
-    settle(sib_copies[3:4])
-    grads_rows(0, 1 - core, rates_sib[...])
-    grads_sum(0)
-    prim0 = prim_first(0)
-
+    halo_k = halo(0) + halo(1)
     settle(py)
     part = pj.at[z, pl.ds(aligned(x, 64), 64), lanes_a]
     px = go([
         same(part, px_send.at[d - 1], px_recv.at[d - 1], along(x, 4, 8, d)) for d in (1, 2, 3)
     ])
+    settle(sib_copies[3:4])
+    grads_rows(0, 1 - core, rates_sib[...])
+    grads_sum(0)
+    prim0 = prim_first(0)
+
+    grads_rows(1, core, rates_ref[...])
+    settle(px)
+    pz0a = pz(0, 0, 0, 0)
+    pz0b = pz(0, 1, 0, 0)
     settle(bz)
     part = pj.at[:, place, lanes_b]
     by = go([
@@ -441,8 +448,6 @@
     ])
     grads_rows(1, 1 - core, rates_sib[...])
     grads_sum(1)
-    settle(px)
-    pz0 = pz(0, 0, 0)
     prim0 = prim_second(0, prim0)
     prim1 = prim_first(1)
     for j in range(2):
@@ -454,48 +459,59 @@
     attend(0, 1)
     prim_last(0, prim0)
     sec0 = sec_sends(0)
-    settle(pz0)
-    pz1 = pz(1, 7, 1)
+    halo_k += halo(2)
+    settle(pz0a)
+    pz1a = pz(1, 0, 7, 1)
     prim1 = prim_second(1, prim1)
+    halo_k += halo(3)
     sec_last(0, sec0)
     z0 = z_sends(0)
     attend(1, 1)
     prim_last(1, prim1)
     sec1 = sec_sends(1)
+    halo_v = halo(4)
+    settle(by)
+    bx0 = bx(0, [(0, 0, x_right), (0, 1, x_left)])
     ag0 = renorm(0, z0)
-    halo_k += halo(1)
-    halo_v = halo(2)
-    settle(by)
-    bx0 = bx(0, [(0, 0, x_right), (0, 1, x_left), (0, 1, x_right), (0, 0, x_left)])
+    halo_v += halo(5)
     sec_last(1, sec1)
     z1 = z_sends(1)
+    halo_v += halo(6)
     unpack(0, ag0)
     ags0 = agsec_sends(0)
+    bx1 = bx(1, [(0, 1, x_right), (0, 0, x_left)])
+    halo_v += halo(7)
     ag1 = renorm(1, z1)
+    settle(pz0b)
+    pz1b = pz(1, 1, 7, 1)
+    settle(pz1a)
+    pz2a = pz(2, 0, 6, 2)
     settle(ags0)
     agp0 = agp_first(0)
-    halo_v += halo(3)
-    settle(pz1)
-    pz2 = pz(2, 6, 2)
     unpack(1, ag1)
     ags1 = agsec_sends(1)
     agp0 = agp_second(0, agp0)
     settle(ags1)
     agp1 = agp_first(1)
     settle(bx0)
-    bx1 = bx(1, [(3, 0, x_right), (1, 1, x_left)])
-    settle(pz2)
-    pz3 = pz(3, 5, 3, 0, 128, 128)
+    bx2 = bx(2, [(3, 0, x_right), (1, 1, x_left)])
+    settle(pz1b)
+    pz2b = pz(2, 1, 6, 2)
+    settle(pz2a)
+    pz3 = pz(3, 0, 5, 3, (0,))
     settle(halo_k)
-    settle(halo_v[:1])
+    settle(halo_v[:2])
     attend(0, 0)
-    settle(halo_v[1:])
+    settle(halo_v[2:])
     attend(1, 0)
+    settle(pz2b)
+    pz3 += pz(3, 1, 5, 3, (1,))
     agp1 = agp_second(1, agp1)
     settle(agp0)
     forward(0)
     settle(pz3)
     settle(bx1)
+    settle(bx2)
 
     their_rows = aligned(1 - core, TOK)
 
@@ -543,8 +559,8 @@
         pltpu.VMEM((2, 512, 512), BF16),
         pltpu.VMEM((2, 512, 512), BF16),
         pltpu.VMEM((6, 512, 512), BF16),
-        pltpu.VMEM((6, 64, 512), BF16),
-        pltpu.VMEM((6, 64, 512), BF16),
+        pltpu.VMEM((6, HALF, 512), BF16),
+        pltpu.VMEM((6, 128 - HALF, 512), BF16),
         pltpu.VMEM((6, 128, 512), BF16),
         pltpu.VMEM((6, 128, 512), BF16),
         pltpu.VMEM((6, 128, 512), BF16),
@@ -570,11 +586,11 @@
         sem((12,)), sem((12,)),
         sem((3,)), sem((3,)),
         sem((3,)), sem((3,)),
-        sem((8,)), sem((8,)),
+        sem((16,)), sem((16,)),
         sem((7,)), sem((7,)),
         sem((3,)), sem((3,)),
         sem((8,)), sem((8,)),
-        sem((4,)), sem((4,)),
+        sem((8,)), sem((8,)),
         sem((4,)), sem((4,)),
     ]
     return pl.pallas_call(

time: 100 us -> 97.4 us (0.974)
  Pallas kernels: 99.3 us -> 96.2 us
    pallas_call x1, Pallas kernels: 99.3 us -> 96.2 us  [body(): pl.pallas_call(kernel, out_shape=pltpu.VMEM((TOK, 2048), BF16), in_specs=...]
where the time goes in v3:
time: 97.4 us; the launch traced here: 97.2 us
  Pallas kernels  96.2 us (99%)
    pallas_call x1, Pallas kernels, body(): pl.pallas_call(kernel, out_shape=pltpu.VMEM((TOK, 2048), BF16), in_specs=...  96.2 us

profile of v3, /device:TPU:1, one launch (start us, length us, event | category | flops | bytes accessed | tf_op | source)
XLA Modules:
  0.0 97.2 jit_solution(8719083701158329996)
XLA Ops:
  0.0 96.2 %shard_map.73 = bf16[256,2048]{1,0:T(8,128)(2,1)S(1)} custom-call(bf16[256,2048]{1,0:T(8,128)(2,1)} %q_hbm.1, bf16[256,2048]{1,0:T(8,128)(2,1)} %k_hbm.1, bf16[256,2048]{1,0:T(8,128)(2,1)} %v_hbm.1, f32[2,128]{1,0:T(2,128)} %bitcast.3, bf16[4,3,512,512]{3,2,1,0:T(8,128)(2,1)} %w_hbm.1, f32[4,512]{1,0:T(4,128)} %gain_ref.1, bf16[8,2048]{1,0:T(8,128)(2,1)} %bitcast.2), custom_call_target="tpu_custom_call" | custom-call | flops 12000000000 | bytes 10000000 | tf_op jit(solution)/shard_map/pallas_call | solution.py:596
  96.2 1.0 %copy.9 = bf16[256,2048]{1,0:T(8,128)(2,1)} copy(bf16[256,2048]{1,0:T(8,128)(2,1)S(1)} %shard_map.73) | data formatting | bytes 2097152

commit v4 on v3

--- a/solution.py
+++ b/solution.py
@@ -424,9 +424,10 @@
 
     for copy in locals_[:3]:
         copy.wait()
+    settle(sib_copies[2:3])
+    halo_all = halo(0) + halo(1)
     grads_rows(0, core, rates_ref[...])
-    settle(sib_copies[1:3])
-    halo_k = halo(0) + halo(1)
+    settle(sib_copies[1:2])
     settle(py)
     part = pj.at[z, pl.ds(aligned(x, 64), 64), lanes_a]
     px = go([
@@ -459,28 +460,28 @@
     attend(0, 1)
     prim_last(0, prim0)
     sec0 = sec_sends(0)
-    halo_k += halo(2)
+    halo_all += halo(2)
     settle(pz0a)
     pz1a = pz(1, 0, 7, 1)
     prim1 = prim_second(1, prim1)
-    halo_k += halo(3)
+    halo_all += halo(3)
     sec_last(0, sec0)
     z0 = z_sends(0)
     attend(1, 1)
     prim_last(1, prim1)
     sec1 = sec_sends(1)
-    halo_v = halo(4)
+    halo_all += halo(4)
+    halo_all += halo(5)
     settle(by)
     bx0 = bx(0, [(0, 0, x_right), (0, 1, x_left)])
     ag0 = renorm(0, z0)
-    halo_v += halo(5)
+    halo_all += halo(6)
     sec_last(1, sec1)
     z1 = z_sends(1)
-    halo_v += halo(6)
+    halo_all += halo(7)
     unpack(0, ag0)
     ags0 = agsec_sends(0)
     bx1 = bx(1, [(0, 1, x_right), (0, 0, x_left)])
-    halo_v += halo(7)
     ag1 = renorm(1, z1)
     settle(pz0b)
     pz1b = pz(1, 1, 7, 1)
@@ -499,10 +500,9 @@
     pz2b = pz(2, 1, 6, 2)
     settle(pz2a)
     pz3 = pz(3, 0, 5, 3, (0,))
-    settle(halo_k)
-    settle(halo_v[:2])
+    settle([halo_all[i] for i in (0, 1, 2, 3, 4, 5)])
     attend(0, 0)
-    settle(halo_v[2:])
+    settle(halo_all[6:])
     attend(1, 0)
     settle(pz2b)
     pz3 += pz(3, 1, 5, 3, (1,))

time: 97.4 us -> 97 us (level)
  Pallas kernels: 96.2 us -> 95.2 us
    pallas_call x1, Pallas kernels: 96.2 us -> 95.2 us  [body(): pl.pallas_call(kernel, out_shape=pltpu.VMEM((TOK, 2048), BF16), in_specs=...]
where the time goes in v4:
time: 97 us; the launch traced here: 96.1 us
  Pallas kernels  95.2 us (98%)
  local copies, waits for them, and re-layouts  0.97 us (1%)
    pallas_call x1, Pallas kernels, body(): pl.pallas_call(kernel, out_shape=pltpu.VMEM((TOK, 2048), BF16), in_specs=...  95.2 us

profile of v4, /device:TPU:1, one launch (start us, length us, event | category | flops | bytes accessed | tf_op | source)
XLA Modules:
  0.0 96.1 jit_solution(12106903088726715715)
XLA Ops:
  0.0 95.2 %shard_map.73 = bf16[256,2048]{1,0:T(8,128)(2,1)S(1)} custom-call(bf16[256,2048]{1,0:T(8,128)(2,1)} %q_hbm.1, bf16[256,2048]{1,0:T(8,128)(2,1)} %k_hbm.1, bf16[256,2048]{1,0:T(8,128)(2,1)} %v_hbm.1, f32[2,128]{1,0:T(2,128)} %bitcast.3, bf16[4,3,512,512]{3,2,1,0:T(8,128)(2,1)} %w_hbm.1, f32[4,512]{1,0:T(4,128)} %gain_ref.1, bf16[8,2048]{1,0:T(8,128)(2,1)} %bitcast.2), custom_call_target="tpu_custom_call" | custom-call | flops 12000000000 | bytes 10000000 | tf_op jit(solution)/shard_map/pallas_call | solution.py:596
  95.2 1.0 %copy.9 = bf16[256,2048]{1,0:T(8,128)(2,1)} copy(bf16[256,2048]{1,0:T(8,128)(2,1)S(1)} %shard_map.73) | data formatting | bytes 2097152
